TPU v7x, 32 devices: a whole 2x2x4 slice. The times are simulated.
32 devices in a mesh: groups: 1, rail: 16 (over z, y, x), node: 2 (over core).
Axes of the slice: x: 2, y: 2, z: 4, core: 2. Of those that a mesh axis runs over, the one named last changes fastest.
Arguments:
- tokens: bfloat16 [512, 7168], P(('groups', 'rail', 'node')), may hold values from -6 to 6
- routes: int32 [512, 2], P(('groups', 'rail', 'node')), may hold values from 0 to 3, all different within a row; in each aligned block of 16 rows (0 to 15, 16 to 31, ...) at most 12 rows name the same one
- route_weight: int32 [512, 2], P(('groups', 'rail', 'node')), may hold values from 1 to 255
- gate_weight: bfloat16 [16, 2, 7168, 256], P('rail', 'node'), may hold values from -0.0625 to 0.0625
- up_weight: bfloat16 [16, 2, 7168, 256], P('rail', 'node'), may hold values from -0.0625 to 0.0625
- down_weight: bfloat16 [16, 2, 256, 7168], P('rail', 'node'), may hold values from -0.125 to 0.125
Outputs:
- moe_out: bfloat16 [512, 7168], P(('groups', 'rail', 'node'))
Inputs may be any that keep to these rules, and one draw needn't show every extreme that they name: `routes`: each row names 2 different experts; among the 16 rows of one device no expert is named by more than 12 rows, and in some blocks of every draw an expert is named by exactly 12.
All inputs are finite; a program needn't handle non-finite values.
Results may differ from a plain program's by a relative error of at most 0.0085.
Values may be sent and summed in bfloat16 or wider, within the bound.
A program may use at most 128 MiB of HBM per device.

v0:
```python
import jax
import jax.numpy as jnp
from jax import lax
from jax.sharding import PartitionSpec as P

SLICES = 8


def partner_2(block, axis, distance):
    count = lax.axis_size(axis)
    route = []
    for low in range(count):
        high = low | 1 << distance
        if high != low and high < count:
            route += [(low, high), (high, low)]
    return lax.ppermute(block, axis, route)


def shards(tokens, routes, route_weight, gate_weight, up_weight, down_weight):
    row_count, model_width = tokens.shape
    top_count = routes.shape[1]
    rail_size = lax.axis_size("rail")
    node_size = lax.axis_size("node")
    devices = rail_size * node_size
    experts = devices // SLICES
    capacity = min(row_count, 3 * row_count * top_count // (2 * experts))
    split_count = rail_size // SLICES
    piece_width = model_width // SLICES
    levels = SLICES.bit_length() - 1
    listed = routes.reshape(-1)
    onehot = (listed[:, None] == jnp.arange(experts, dtype=jnp.int32)[None, :]).astype(jnp.int32)
    earlier = jnp.cumsum(onehot, axis=0) - onehot
    slot_key = listed * capacity + jnp.sum(earlier * onehot, axis=1)
    chosen = slot_key[:, None] == jnp.arange(experts * capacity, dtype=jnp.int32)[None, :]
    chosen = chosen.reshape(row_count, top_count, experts * capacity)
    dispatch = jnp.sum(chosen.astype(jnp.bfloat16), axis=1)
    share = route_weight.astype(jnp.float32) / 256.0
    combine = jnp.sum(chosen.astype(jnp.float32) * share[:, :, None], axis=1)
    packed = jnp.einsum("te,td->ed", dispatch, tokens, preferred_element_type=jnp.float32).astype(
        jnp.bfloat16
    )
    w_gate = gate_weight[0, 0]
    w_up = up_weight[0, 0]
    w_down = down_weight[0, 0]
    rail_index = lax.axis_index("rail")

    def own_bit(bit):
        return rail_index // 2**bit % 2 == 1

    pieces = packed.reshape(split_count, node_size, capacity, SLICES, piece_width)
    pieces = pieces.transpose(0, 3, 1, 2, 4).reshape(devices, capacity, piece_width)
    assembled = lax.all_to_all(pieces, ("rail", "node"), split_axis=0, concat_axis=0, tiled=True)
    for bit in range(levels):
        partner = partner_2(assembled, "rail", bit)
        assembled = jnp.where(
            own_bit(bit),
            jnp.concatenate([partner, assembled], 2),
            jnp.concatenate([assembled, partner], 2),
        )
    rows = assembled.reshape(-1, model_width)
    gate_vals = jnp.dot(rows, w_gate, preferred_element_type=jnp.float32)
    up_vals = jnp.dot(rows, w_up, preferred_element_type=jnp.float32)
    hidden = (jax.nn.silu(gate_vals) * up_vals).astype(jnp.bfloat16)
    partial_value = jnp.dot(hidden, w_down, preferred_element_type=jnp.float32)
    partials = partial_value.reshape(assembled.shape)
    half = model_width // 2
    upper = own_bit(levels - 1)
    lower_part = partials[:, :, :half]
    upper_part = partials[:, :, half:]
    sending = jnp.where(upper, lower_part, upper_part)
    keeping = jnp.where(upper, upper_part, lower_part)
    received = partner_2(sending, "rail", levels - 1)
    current = keeping + received
    for bit in range(levels - 2, -1, -1):
        half = current.shape[2] // 2
        upper = own_bit(bit)
        lower_part = current[:, :, :half]
        upper_part = current[:, :, half:]
        sending = jnp.where(upper, lower_part, upper_part)
        keeping = jnp.where(upper, upper_part, lower_part)
        received = partner_2(sending, "rail", bit)
        current = keeping + received
    returned = lax.all_to_all(current, ("rail", "node"), split_axis=0, concat_axis=0, tiled=True)
    summed = returned.reshape(split_count, SLICES, node_size, capacity, piece_width)
    summed = summed.transpose(0, 2, 3, 1, 4).reshape(experts * capacity, model_width)
    mixed = jnp.dot(
        combine, summed, precision=lax.Precision.HIGHEST, preferred_element_type=jnp.float32
    )
    return mixed.astype(jnp.bfloat16)


def solution(mesh):
    in_specs = (
        P(("groups", "rail", "node"), None),
        P(("groups", "rail", "node"), None),
        P(("groups", "rail", "node"), None),
        P("rail", "node", None, None),
        P("rail", "node", None, None),
        P("rail", "node", None, None),
    )
    out_specs = P(("groups", "rail", "node"), None)
    return jax.shard_map(shards, mesh=mesh, in_specs=in_specs, out_specs=out_specs, check_vma=False)
```

profile of v0, /device:TPU:0, one launch (start us, length us, event | category | flops | bytes accessed | tf_op | source)
XLA Modules:
  0.0 447.1 jit_solution(17365011079022647936)
XLA Ops:
  3.4 30.5 %all_to_all.10 = bf16[32,12,896]{2,1,0:T(8,128)(2,1)S(1)} all-to-all(bf16[32,12,896]{2,1,0:T(8,128)(2,1)S(1)} %bitcast.32), channel_id=1, replica_groups=mesh['groups'=1,'rail'=16,'node'=2] {'rail','node'}, dimensions={0} | all-to-all | bytes 1376256 | tf_op jit(solution)/shard_map/all_to_all | solution.py:52
  34.0 1.5 collective-permute-start
  35.6 15.6 %collective-permute-done = bf16[32,12,896]{2,0,1:T(8,128)(2,1)S(1)} collective-permute-done((bf16[32,12,896]{2,0,1:T(8,128)(2,1)S(1)}, bf16[32,12,896]{2,0,1:T(8,128)(2,1)S(1)}, u32[]{:S(2)}, u32[]{:S(2)}) %collective-permute-start) | collective-permute-done | bytes 688160 | tf_op jit(solution)/shard_map/ppermute | solution.py:16
  55.1 29.6 %collective-permute-done.1 = bf16[32,12,1792]{2,0,1:T(8,128)(2,1)} collective-permute-done((bf16[32,12,1792]{2,0,1:T(8,128)(2,1)S(1)}, bf16[32,12,1792]{2,0,1:T(8,128)(2,1)}, u32[]{:S(2)}, u32[]{:S(2)}) %collective-permute-start.1) | collective-permute-done | bytes 1376288 | tf_op jit(solution)/shard_map/ppermute | solution.py:16
  84.7 2.1 copy.78
  88.0 3.1 copy.80
  91.0 1.9 collective-permute-start.2
  97.1 4.5 %maximum_select_fusion.2 = bf16[384,3584]{1,0:T(8,128)(2,1)} fusion(bf16[384,1792]{1,0:T(8,128)(2,1)} %maximum_select_fusion.4, bf16[384,1792]{1,0:T(8,128)(2,1)} %concatenate.45, pred[]{:T(512)S(6)} %eq.56), kind=kLoop, calls=%fused_computation.12 | loop fusion | flops 12386304 | bytes 5505025 | tf_op jit(solution)/shard_map/jit(_where)/select_n | solution.py:55
  101.6 49.8 %collective-permute-done.2 = bf16[32,12,3584]{2,0,1:T(8,128)(2,1)} collective-permute-done((bf16[32,12,3584]{2,0,1:T(8,128)(2,1)}, bf16[32,12,3584]{2,0,1:T(8,128)(2,1)}, u32[]{:S(2)}, u32[]{:S(2)}) %collective-permute-start.2) | collective-permute-done | bytes 2752544 | tf_op jit(solution)/shard_map/ppermute | solution.py:16
  151.4 5.2 %copy.81 = bf16[32,12,3584]{2,1,0:T(8,128)(2,1)} copy(bf16[32,12,3584]{2,0,1:T(8,128)(2,1)} %collective-permute-done.2) | data formatting | bytes 5505024 | tf_op jit(solution)/shard_map/ppermute | solution.py:16
  156.6 5.4 %concatenate.44 = bf16[384,3584]{1,0:T(8,128)(2,1)} reshape(bf16[32,12,3584]{2,1,0:T(8,128)(2,1)} %copy.81) | data formatting | bytes 5505024 | tf_op jit(solution)/shard_map/concatenate | solution.py:57
  162.0 6.4 %fusion.4 = f32[384,256]{1,0:T(8,128)S(1)} fusion(bf16[1,1,7168,256]{3,2,1,0:T(8,128)(2,1)} %param.9, bf16[384,3584]{1,0:T(8,128)(2,1)} %maximum_select_fusion.2, bf16[384,3584]{1,0:T(8,128)(2,1)} %concatenate.44, pred[]{:T(512)S(6)} %eq.57), kind=kOutput, calls=%fused_computation.10 | convolution fusion | flops 1434058752 | bytes 9568257 | tf_op jit(solution)/shard_map/dot_general | solution.py:61
  169.9 3.1 multiply_convert_fusion
  173.0 3.6 fusion
  177.5 1.8 collective-permute-start.3
  179.4 116.5 %collective-permute-done.3 = f32[32,12,3584]{2,0,1:T(8,128)} collective-permute-done((f32[32,12,3584]{2,0,1:T(8,128)S(1)}, f32[32,12,3584]{2,0,1:T(8,128)}, u32[]{:S(2)}, u32[]{:S(2)}) %collective-permute-start.3) | collective-permute-done | bytes 5505056 | tf_op jit(solution)/shard_map/ppermute | solution.py:16
  295.8 6.6 %select_add_fusion = f32[32,12,3584]{2,0,1:T(8,128)} fusion(f32[32,12,3584]{2,0,1:T(8,128)} %collective-permute-done.3, f32[32,12,7168]{2,0,1:T(8,128)S(1)} %fusion, pred[]{:T(512)S(6)} %eq.57), kind=kLoop, calls=%fused_computation.3 | loop fusion | flops 2752512 | bytes 22020096 | tf_op jit(solution)/shard_map/add | solution.py:73
  302.5 3.1 slice_select_fusion.1
  306.4 57.5 %collective-permute-done.4 = f32[32,12,1792]{2,0,1:T(8,128)S(1)} collective-permute-done((f32[32,12,1792]{2,0,1:T(8,128)S(1)}, f32[32,12,1792]{2,0,1:T(8,128)S(1)}, u32[]{:S(2)}, u32[]{:S(2)}) %collective-permute-start.4) | collective-permute-done | bytes 2752544 | tf_op jit(solution)/shard_map/ppermute | solution.py:16
  364.5 3.6 collective-permute-start.5
  368.2 26.6 %collective-permute-done.5 = f32[32,12,896]{2,0,1:T(8,128)S(1)} collective-permute-done((f32[32,12,896]{2,0,1:T(8,128)S(1)}, f32[32,12,896]{2,0,1:T(8,128)S(1)}, u32[]{:S(2)}, u32[]{:S(2)}) %collective-permute-start.5) | collective-permute-done | bytes 1376288 | tf_op jit(solution)/shard_map/ppermute | solution.py:16
  395.0 2.1 copy.85
  397.1 4.3 all-to-all-start.1
  401.5 43.1 %all-to-all-done.1 = f32[32,12,896]{2,1,0:T(8,128)S(1)} async-done(((f32[32,12,896]{2,1,0:T(8,128)}), f32[32,12,896]{2,1,0:T(8,128)S(1)}, u32[]{:S(2)}, u32[]{:S(2)}) %all-to-all-start.1) | async-done | bytes 1376288 | tf_op jit(solution)/shard_map/all_to_all | solution.py:83
  (54 shorter events, 19.4 us)
Async XLA Ops:
  0.0 2.2 copy-start
  34.0 17.1 %collective-permute-start = (bf16[32,12,896]{2,0,1:T(8,128)(2,1)S(1)}, bf16[32,12,896]{2,0,1:T(8,128)(2,1)S(1)}, u32[]{:S(2)}, u32[]{:S(2)}) collective-permute-start(bf16[32,12,896]{2,0,1:T(8,128)(2,1)S(1)} %copy.74), channel_id=1, source_target_pairs={{0,2},{2,0},{4,6},{6,4},{8,10},{10,8},{12,14},{14,12},{16,18},{18,... | collective-permute-start | bytes 2064392 | tf_op jit(solution)/shard_map/ppermute | solution.py:16
  51.4 2.2 copy-start.5
  51.9 1.2 copy-start.3
  53.6 31.1 %collective-permute-start.1 = (bf16[32,12,1792]{2,0,1:T(8,128)(2,1)S(1)}, bf16[32,12,1792]{2,0,1:T(8,128)(2,1)}, u32[]{:S(2)}, u32[]{:S(2)}) collective-permute-start(bf16[32,12,1792]{2,0,1:T(8,128)(2,1)S(1)} %copy.77), channel_id=1, source_target_pairs={{0,4},{4,0},{2,6},{6,2},{8,12},{12,8},{10,14},{14,10},{16,20},{20,... | collective-permute-start | bytes 4128776 | tf_op jit(solution)/shard_map/ppermute | solution.py:16
  55.1 31.7 %copy-start.4 = (bf16[32,12,1792]{2,1,0:T(8,128)(2,1)S(1)}, bf16[32,12,1792]{2,1,0:T(8,128)(2,1)}, u32[]{:S(2)}) copy-start(bf16[32,12,1792]{2,1,0:T(8,128)(2,1)} %copy-done.3) | copy-start | bytes 4128772
  91.0 60.4 %collective-permute-start.2 = (bf16[32,12,3584]{2,0,1:T(8,128)(2,1)}, bf16[32,12,3584]{2,0,1:T(8,128)(2,1)}, u32[]{:S(2)}, u32[]{:S(2)}) collective-permute-start(bf16[32,12,3584]{2,0,1:T(8,128)(2,1)} %copy.80), channel_id=1, source_target_pairs={{0,8},{8,0},{2,10},{10,2},{4,12},{12,4},{6,14},{14,6},{16,24},{24,... | collective-permute-start | bytes 8257544 | tf_op jit(solution)/shard_map/ppermute | solution.py:16
  162.0 6.4 %copy-start.6 = (bf16[384,3584]{1,0:T(8,128)(2,1)S(1)}, bf16[384,3584]{1,0:T(8,128)(2,1)}, u32[]{:S(2)}) copy-start(bf16[384,3584]{1,0:T(8,128)(2,1)} %maximum_select_fusion.2) | copy-start | bytes 8257540
  162.0 6.9 %copy-start.7 = (bf16[384,3584]{1,0:T(8,128)(2,1)S(1)}, bf16[384,3584]{1,0:T(8,128)(2,1)}, u32[]{:S(2)}) copy-start(bf16[384,3584]{1,0:T(8,128)(2,1)} %concatenate.44) | copy-start | bytes 8257540
  162.0 7.9 %copy-start.9 = (bf16[1,1,7168,256]{3,2,1,0:T(8,128)(2,1)S(1)}, bf16[1,1,7168,256]{3,2,1,0:T(8,128)(2,1)}, u32[]{:S(2)}) copy-start(bf16[1,1,7168,256]{3,2,1,0:T(8,128)(2,1)} %param.10) | copy-start | bytes 11010052
  177.5 118.3 %collective-permute-start.3 = (f32[32,12,3584]{2,0,1:T(8,128)S(1)}, f32[32,12,3584]{2,0,1:T(8,128)}, u32[]{:S(2)}, u32[]{:S(2)}) collective-permute-start(f32[32,12,3584]{2,0,1:T(8,128)S(1)} %slice_select_fusion), channel_id=1, source_target_pairs={{0,8},{8,0},{2,10},{10,2},{4,12},{12,4},{6,14},{14,6},{16,24},{24,... | collective-permute-start | bytes 16515080 | tf_op jit(solution)/shard_map/ppermute | solution.py:16
  302.5 61.4 %copy-start.2 = (f32[32,12,3584]{2,0,1:T(8,128)S(1)}, f32[32,12,3584]{2,0,1:T(8,128)}, u32[]{:S(2)}) copy-start(f32[32,12,3584]{2,0,1:T(8,128)} %select_add_fusion) | copy-start | bytes 16515076
  305.6 58.3 %collective-permute-start.4 = (f32[32,12,1792]{2,0,1:T(8,128)S(1)}, f32[32,12,1792]{2,0,1:T(8,128)S(1)}, u32[]{:S(2)}, u32[]{:S(2)}) collective-permute-start(f32[32,12,1792]{2,0,1:T(8,128)S(1)} %slice_select_fusion.1), channel_id=1, source_target_pairs={{0,4},{4,0},{2,6},{6,2},{8,12},{12,8},{10,14},{14,10},{16,20},{20,... | collective-permute-start | bytes 8257544 | tf_op jit(solution)/shard_map/ppermute | solution.py:16
  364.5 30.2 %collective-permute-start.5 = (f32[32,12,896]{2,0,1:T(8,128)S(1)}, f32[32,12,896]{2,0,1:T(8,128)S(1)}, u32[]{:S(2)}, u32[]{:S(2)}) collective-permute-start(f32[32,12,896]{2,0,1:T(8,128)S(1)} %slice_select_fusion.2), channel_id=1, source_target_pairs={{0,2},{2,0},{4,6},{6,4},{8,10},{10,8},{12,14},{14,12},{16,18},{18,... | collective-permute-start | bytes 4128776 | tf_op jit(solution)/shard_map/ppermute | solution.py:16
  395.0 6.4 %copy-start.8 = (s32[16,2]{0,1:T(2,128)S(1)}, s32[16,2]{0,1:T(2,128)}, u32[]{:S(2)}) copy-start(s32[16,2]{0,1:T(2,128)} %param.8) | copy-start | bytes 388
  397.1 47.5 %all-to-all-start.1 = ((f32[32,12,896]{2,1,0:T(8,128)}), f32[32,12,896]{2,1,0:T(8,128)S(1)}, u32[]{:S(2)}, u32[]{:S(2)}) async-start(f32[32,12,896]{2,1,0:T(8,128)} %copy.85), calls=%async_computation.1 | async-start | bytes 3670016 | tf_op jit(solution)/shard_map/all_to_all | solution.py:83
  444.6 2.5 copy-start.1
where the time goes:
time: 448 us; the launch traced here: 447 us
  waiting for transfers between devices  339 us (76%)
  blocking collectives  30.5 us (7%)
  local copies, waits for them, and re-layouts  27 us (6%)
  other arithmetic  20.3 us (5%)
  starting transfers between devices  15.4 us (3%)
  matrix products  14.9 us (3%)
    ppermute x6, waiting for transfers between devices, partner_2(): return lax.ppermute(block, axis, route)  296 us
    all_to_all x1, waiting for transfers between devices, shards(): lax.all_to_all(current, ('rail', 'node'), split_axis=0, concat_axis=0, ti...  43.1 us
    all_to_all x1, blocking collectives, shards(): lax.all_to_all(pieces, ('rail', 'node'), split_axis=0, concat_axis=0, til...  30.5 us
    ppermute x6, starting transfers between devices, partner_2(): return lax.ppermute(block, axis, route)  11.1 us
  transfers between devices with their start and end apart: 7, of which 7 were waited for; matrix products, arithmetic and copies ran while one was open for 2% of the time, Pallas kernels for 0%

commit v1 on v0

v1 whole, which is shorter than its diff:
```python
import functools

import jax
import jax.numpy as jnp
from jax import lax
from jax.experimental import pallas as pl
from jax.experimental.pallas import tpu as pltpu
from jax.sharding import PartitionSpec as P

SLICES = 8
SQUARE = 4
LANES = 128


def body(
    rail_size,
    node_size,
    tokens_ref,
    routes_ref,
    weight_ref,
    gate_hbm,
    up_hbm,
    down_hbm,
    out_ref,
    rows_ref,
    gate_ref,
    up_ref,
    down_ref,
    sib_buf,
    side_buf,
    line_buf,
    above_buf,
    below_buf,
    load_sem,
    chain_send,
    chain_recv,
    first_send,
    first_recv,
    second_send,
    second_recv,
    relay_send,
    relay_recv,
    sib_send,
    sib_recv,
    give_send,
    give_recv,
    side_send,
    side_recv,
    line_send,
    line_recv,
    sum_send,
    above_recv,
    below_recv,
):
    count, width = tokens_ref.shape
    middle = width // LANES // 2 * LANES
    depth = rail_size // SQUARE
    rail = lax.axis_index("rail")
    node = lax.axis_index("node")
    x, y, z = lax.rem(rail, 2), lax.rem(rail // 2, 2), rail // SQUARE
    expert = rail // SLICES * node_size + node
    to_sib = {"node": 1 - node}
    to_x = {"rail": rail + 1 - 2 * x}
    to_y = {"rail": rail + 2 - 4 * y}
    to_above = {"rail": rail + SQUARE}
    to_below = {"rail": rail - SQUARE}
    has_above = z < depth - 1
    has_below = z > 0
    steps = 2 * depth - 1

    def index_of(zz, flip_x, flip_y):
        xx = 1 - x if flip_x else x
        yy = 1 - y if flip_y else y
        return zz * SQUARE + yy * 2 + xx

    def band(i):
        return pl.ds(pl.multiple_of(i * count, count), count)

    full = slice(0, width + LANES)
    plain = slice(0, width)
    halves_wide = (slice(0, middle), slice(middle, width + LANES))
    halves = (slice(0, middle), slice(middle, width))

    def rows_at(r, n, columns):
        return rows_ref.at[band(r * node_size + n), columns]

    def copy(src, dst, send, recv, target):
        return pltpu.make_async_remote_copy(
            src_ref=src,
            dst_ref=dst,
            send_sem=send,
            recv_sem=recv,
            device_id=target,
            device_id_type=pl.DeviceIdType.MESH,
        )

    loads = [
        pltpu.make_async_copy(hbm.at[0, 0], ref, load_sem.at[i])
        for i, (hbm, ref) in enumerate(
            ((gate_hbm, gate_ref), (up_hbm, up_ref), (down_hbm, down_ref))
        )
    ]

    barrier = pltpu.get_barrier_semaphore()
    for target in (to_sib, to_x, to_y):
        pl.semaphore_signal(barrier, inc=1, device_id=target, device_id_type=pl.DeviceIdType.MESH)

    @pl.when(has_above)
    def _():
        pl.semaphore_signal(
            barrier, inc=1, device_id=to_above, device_id_type=pl.DeviceIdType.MESH
        )

    @pl.when(has_below)
    def _():
        pl.semaphore_signal(
            barrier, inc=1, device_id=to_below, device_id_type=pl.DeviceIdType.MESH
        )

    own = band(rail * node_size + node)
    rows_ref[own, plain] = tokens_ref[...]
    lane = lax.broadcasted_iota(jnp.int32, (count, LANES), 1)
    named = jnp.zeros((count, LANES), jnp.float32)
    for k in range(routes_ref.shape[1]):
        named += jnp.where(
            lane == routes_ref[:, k : k + 1], weight_ref[:, k : k + 1].astype(jnp.float32), 0.0
        )
    rows_ref[own, slice(width, width + LANES)] = named.astype(jnp.bfloat16)
    pl.semaphore_wait(barrier, 3 + has_above.astype(jnp.int32) + has_below.astype(jnp.int32))

    def place(q):
        half = (q + 1) // 2
        return jnp.where(lax.rem(q, 2) == 1, z - half, z + half)

    def visit(q, work):
        zz = place(q)

        @pl.when((q >= 0) & (q < steps) & (zz >= 0) & (zz < depth))
        def _():
            work(zz)

    def chain_up(zz):
        piece = rows_at(index_of(zz, 0, 0), node, full)
        return copy(piece, piece, chain_send.at[0, zz], chain_recv.at[zz], to_above)

    def chain_down(zz):
        piece = rows_at(index_of(zz, 0, 0), node, full)
        return copy(piece, piece, chain_send.at[1, zz], chain_recv.at[zz], to_below)

    def first(zz, h):
        piece = rows_at(index_of(zz, 0, 0), node, halves_wide[h])
        return copy(
            piece, piece, first_send.at[zz, h], first_recv.at[zz, h], (to_x, to_y)[h]
        )

    def first_in(zz, h):
        piece = rows_at(index_of(zz, h == 0, h == 1), node, halves_wide[h])
        return copy(
            piece, piece, first_send.at[zz, h], first_recv.at[zz, h], (to_x, to_y)[h]
        )

    def second(zz, h):
        piece = rows_at(index_of(zz, 0, 0), node, halves_wide[h])
        return copy(
            piece, piece, second_send.at[zz, h], second_recv.at[zz, h], (to_y, to_x)[h]
        )

    def second_in(zz, h):
        piece = rows_at(index_of(zz, h == 1, h == 0), node, halves_wide[h])
        return copy(
            piece, piece, second_send.at[zz, h], second_recv.at[zz, h], (to_y, to_x)[h]
        )

    def relay(zz, h):
        piece = rows_at(index_of(zz, h == 0, h == 1), node, halves_wide[h])
        return copy(
            piece, piece, relay_send.at[zz, h], relay_recv.at[zz, h], (to_y, to_x)[h]
        )

    def relay_in(zz, h):
        piece = rows_at(index_of(zz, 1, 1), node, halves_wide[h])
        return copy(
            piece, piece, relay_send.at[zz, h], relay_recv.at[zz, h], (to_y, to_x)[h]
        )

    def sibling(r):
        piece = rows_at(r, node, full)
        return copy(piece, piece, sib_send.at[r], sib_recv.at[r], to_sib)

    def sibling_in(r):
        piece = rows_at(r, 1 - node, full)
        return copy(piece, piece, sib_send.at[r], sib_recv.at[r], to_sib)

    def gather_a(zz):
        @pl.when(zz != z)
        def _():
            chain_up(zz).wait_recv()

        @pl.when((zz <= z) & has_above)
        def _():
            chain_up(zz).start()

        @pl.when((zz >= z) & has_below)
        def _():
            chain_down(zz).start()

        for h in range(2):
            first(zz, h).start()
        for h in range(2):
            second(zz, h).start()
        sibling(index_of(zz, 0, 0)).start()

    def gather_b(zz):
        for h in range(2):
            first_in(zz, h).wait_recv()
            relay(zz, h).start()

    def gather_c(zz):
        for h in range(2):
            second_in(zz, h).wait_recv()
        sibling(index_of(zz, 0, 1)).start()
        sibling(index_of(zz, 1, 0)).start()
        for h in range(2):
            relay_in(zz, h).wait_recv()
        sibling(index_of(zz, 1, 1)).start()

    def gather_step(t, carry):
        visit(t, gather_a)

        @pl.when(t == 0)
        def _():
            for load in loads:
                load.start()

        visit(t - 2, gather_b)
        visit(t - 4, gather_c)
        return carry

    lax.fori_loop(0, steps + 4, gather_step, 0)

    def gather_end(zz, carry):
        @pl.when((zz <= z) & has_above)
        def _():
            chain_up(zz).wait_send()

        @pl.when((zz >= z) & has_below)
        def _():
            chain_down(zz).wait_send()

        for h in range(2):
            first(zz, h).wait_send()
            second(zz, h).wait_send()
            relay(zz, h).wait_send()
        for fx, fy in ((0, 0), (0, 1), (1, 0), (1, 1)):
            r = index_of(zz, fx, fy)
            sibling(r).wait_send()
            sibling_in(r).wait_recv()
        return carry

    lax.fori_loop(0, depth, gather_end, 0)
    for load in loads:
        load.wait()

    total = rail_size * node_size * count
    chunk = min(128, total)
    column_step = next(s for s in (1792, 1024, 512, 256, 128) if width % s == 0)

    def compute(i, carry):
        here = pl.ds(pl.multiple_of(i * chunk, chunk), chunk)
        lane = lax.broadcasted_iota(jnp.int32, (chunk, LANES), 1)
        marks = rows_ref[here, slice(width, width + LANES)].astype(jnp.float32)
        share = jnp.sum(jnp.where(lane == expert, marks, 0.0), axis=1, keepdims=True) / 256.0
        block = rows_ref[here, plain]
        gate = jnp.dot(block, gate_ref[...], preferred_element_type=jnp.float32)
        up = jnp.dot(block, up_ref[...], preferred_element_type=jnp.float32)
        hidden = gate / (1.0 + jnp.exp(-gate)) * up * share
        hidden = hidden.astype(jnp.bfloat16)
        for low in range(0, width, column_step):
            columns = slice(low, low + column_step)
            rows_ref[here, columns] = jnp.dot(
                hidden, down_ref[:, columns], preferred_element_type=jnp.float32
            ).astype(jnp.bfloat16)
        return carry

    lax.fori_loop(0, total // chunk, compute, 0)

    def give(r):
        return copy(
            rows_at(r, 1 - node, plain),
            sib_buf.at[band(r), :],
            give_send.at[r],
            give_recv.at[r],
            to_sib,
        )

    def side(r, h):
        return copy(
            rows_at(r, node, halves[h]),
            side_buf.at[band(r), halves[h]],
            side_send.at[r, h],
            side_recv.at[r, h],
            (to_y, to_x)[h],
        )

    def line(zz, h):
        return copy(
            rows_at(index_of(zz, h == 0, h == 1), node, halves[h]),
            line_buf.at[band(zz), halves[h]],
            line_send.at[zz, h],
            line_recv.at[zz, h],
            (to_x, to_y)[h],
        )

    def sum_up(zz):
        return copy(
            rows_at(index_of(zz, 0, 0), node, plain),
            above_buf.at[band(zz), :],
            sum_send.at[zz],
            above_recv.at[zz],
            to_above,
        )

    def sum_down(zz):
        return copy(
            rows_at(index_of(zz, 0, 0), node, plain),
            below_buf.at[band(zz), :],
            sum_send.at[zz],
            below_recv.at[zz],
            to_below,
        )

    def add(r, columns, other):
        where = band(r * node_size + node)
        rows_ref[where, columns] = (
            rows_ref[where, columns].astype(jnp.float32) + other.astype(jnp.float32)
        ).astype(jnp.bfloat16)

    corners = ((1, 1), (0, 1), (1, 0), (0, 0))

    def reduce_0(zz):
        for fx, fy in corners:
            give(index_of(zz, fx, fy)).start()

    def reduce_a(zz):
        for fx, fy in corners:
            r = index_of(zz, fx, fy)
            give(r).wait_recv()
            add(r, plain, sib_buf[band(r), :])
            if fy:
                side(r, 0).start()
            if fx:
                side(r, 1).start()

    def reduce_b(zz):
        for h in range(2):
            r = index_of(zz, h == 0, h == 1)
            side(r, h).wait_recv()
            add(r, halves[h], side_buf[band(r), halves[h]])
            line(zz, h).start()
        r = index_of(zz, 0, 0)
        for h in range(2):
            side(r, h).wait_recv()
            add(r, halves[h], side_buf[band(r), halves[h]])

    def reduce_c(zz):
        for h in range(2):
            line(zz, h).wait_recv()
        r = index_of(zz, 0, 0)
        add(r, plain, line_buf[band(zz), :])

        @pl.when((zz >= z) & has_below)
        def _():
            sum_up(zz).wait_recv()
            add(r, plain, above_buf[band(zz), :])

        @pl.when((zz <= z) & has_above)
        def _():
            sum_down(zz).wait_recv()
            add(r, plain, below_buf[band(zz), :])

        @pl.when(zz > z)
        def _():
            sum_up(zz).start()

        @pl.when(zz < z)
        def _():
            sum_down(zz).start()

    def reduce_0_step(t, carry):
        visit(steps - 1 - t, reduce_0)
        return carry

    lax.fori_loop(0, steps, reduce_0_step, 0)

    def reduce_step(t, carry):
        q = steps - 1 - t
        visit(q, reduce_a)
        visit(q + 2, reduce_b)
        visit(q + 4, reduce_c)
        return carry

    lax.fori_loop(0, steps + 4, reduce_step, 0)
    out_ref[...] = rows_ref[own, plain]

    def reduce_end(zz, carry):
        for fx, fy in corners:
            r = index_of(zz, fx, fy)
            give(r).wait_send()
            if fy:
                side(r, 0).wait_send()
            if fx:
                side(r, 1).wait_send()
        for h in range(2):
            line(zz, h).wait_send()

        @pl.when(zz > z)
        def _():
            sum_up(zz).wait_send()

        @pl.when(zz < z)
        def _():
            sum_down(zz).wait_send()

        return carry

    lax.fori_loop(0, depth, reduce_end, 0)


def shards(rail_size, node_size, tokens, routes, route_weight, gate, up, down):
    count, width = tokens.shape
    hidden = gate.shape[-1]
    depth = rail_size // SQUARE
    total = rail_size * node_size * count
    bf16 = jnp.bfloat16
    dma = pltpu.SemaphoreType.DMA
    vmem = pl.BlockSpec(memory_space=pltpu.VMEM)
    hbm = pl.BlockSpec(memory_space=pl.ANY)
    return pl.pallas_call(
        functools.partial(body, rail_size, node_size),
        out_shape=jax.ShapeDtypeStruct((count, width), bf16),
        in_specs=[vmem] * 3 + [hbm] * 3,
        out_specs=vmem,
        scratch_shapes=[
            pltpu.VMEM((total, width + LANES), bf16),
            pltpu.VMEM((width, hidden), bf16),
            pltpu.VMEM((width, hidden), bf16),
            pltpu.VMEM((hidden, width), bf16),
            pltpu.VMEM((rail_size * count, width), bf16),
            pltpu.VMEM((rail_size * count, width), bf16),
            pltpu.VMEM((depth * count, width), bf16),
            pltpu.VMEM((depth * count, width), bf16),
            pltpu.VMEM((depth * count, width), bf16),
            dma((3,)),
            dma((2, depth)),
            dma((depth,)),
            dma((depth, 2)),
            dma((depth, 2)),
            dma((depth, 2)),
            dma((depth, 2)),
            dma((depth, 2)),
            dma((depth, 2)),
            dma((rail_size,)),
            dma((rail_size,)),
            dma((rail_size,)),
            dma((rail_size,)),
            dma((rail_size, 2)),
            dma((rail_size, 2)),
            dma((depth, 2)),
            dma((depth, 2)),
            dma((depth,)),
            dma((depth,)),
            dma((depth,)),
        ],
        compiler_params=pltpu.CompilerParams(
            collective_id=0, has_side_effects=True, vmem_limit_bytes=56 * 1024 * 1024
        ),
        cost_estimate=pl.CostEstimate(
            flops=6 * total * width * hidden,
            bytes_accessed=6 * width * hidden,
            transcendentals=total * hidden,
        ),
    )(tokens, routes, route_weight, gate, up, down)


def solution(mesh):
    in_specs = (
        P(("groups", "rail", "node"), None),
        P(("groups", "rail", "node"), None),
        P(("groups", "rail", "node"), None),
        P("rail", "node", None, None),
        P("rail", "node", None, None),
        P("rail", "node", None, None),
    )
    out_specs = P(("groups", "rail", "node"), None)
    work = functools.partial(shards, mesh.shape["rail"], mesh.shape["node"])
    return jax.shard_map(work, mesh=mesh, in_specs=in_specs, out_specs=out_specs, check_vma=False)
```

time: 448 us -> 90 us (0.20)
  waiting for transfers between devices: 339 us -> 0 us
  Pallas kernels: 0 us -> 85.4 us
  blocking collectives: 30.5 us -> 0 us
  local copies, waits for them, and re-layouts: 27 us -> 4.34 us
  other arithmetic: 20.3 us -> 0 us
  starting transfers between devices: 15.4 us -> 0 us
  matrix products: 14.9 us -> 0 us
    ppermute x6 -> x0, waiting for transfers between devices: 296 us -> none  [partner_2(): return lax.ppermute(block, axis, route)]
    pallas_call x0 -> x1, Pallas kernels: none -> 85.4 us  [shards(): pl.pallas_call(functools.partial(body, rail_size, node_size), out_shape=j...]
    all_to_all x1 -> x0, waiting for transfers between devices: 43.1 us -> none  [shards(): lax.all_to_all(current, ('rail', 'node'), split_axis=0, concat_axis=0, ti...]
    all_to_all x1 -> x0, blocking collectives: 30.5 us -> none  [shards(): lax.all_to_all(pieces, ('rail', 'node'), split_axis=0, concat_axis=0, til...]
    dot_general x5 -> x0, matrix products: 14.9 us -> none  [the longest x1 6.41 us: shards(): gate_vals = jnp.dot(rows, w_gate, preferred_element_type=jnp.float32)]
    select_n x7 -> x0, other arithmetic: 11.8 us -> none  [the longest x4 7.7 us: shards(): jnp.where(own_bit(bit), jnp.concatenate([partner, assembled], 2), jnp.con...]
    ppermute x6 -> x0, starting transfers between devices: 11.1 us -> none  [partner_2(): return lax.ppermute(block, axis, route)]
    concatenate x4 -> x0, local copies, waits for them, and re-layouts: 8.07 us -> none  [shards(): jnp.concatenate([partner, assembled], 2)]
  transfers between devices with their start and end apart: 7 -> 0, of which waited for: 7 -> 0; matrix products, arithmetic and copies ran while one was open for 2% -> 0% of each run, Pallas kernels for 0% -> 0%
where the time goes in v1:
time: 90 us; the launch traced here: 89.8 us
  Pallas kernels  85.4 us (95%)
  local copies, waits for them, and re-layouts  4.34 us (5%)
    pallas_call x1, Pallas kernels, shards(): pl.pallas_call(functools.partial(body, rail_size, node_size), out_shape=j...  85.4 us
    unnamed x3, local copies, waits for them, and re-layouts  4.34 us

profile of v1, /device:TPU:0, one launch (start us, length us, event | category | flops | bytes accessed | tf_op | source)
XLA Modules:
  0.0 89.8 jit_solution(13171432808078513624)
XLA Ops:
  0.0 1.4 %copy.7.routes_ref = s32[16,2]{1,0:T(8,128)} copy(s32[16,2]{0,1:T(2,128)} %param.7) | data formatting | bytes 256 | tf_op args[1]
  1.4 1.4 %copy.8.weight_ref = s32[16,2]{1,0:T(8,128)} copy(s32[16,2]{0,1:T(2,128)} %param.8) | data formatting | bytes 256 | tf_op args[2]
  2.7 85.4 %shard_map.64 = bf16[16,7168]{1,0:T(8,128)(2,1)} custom-call(bf16[16,7168]{1,0:T(8,128)(2,1)} %tokens_ref.1, s32[16,2]{1,0:T(8,128)} %copy.7.routes_ref, s32[16,2]{1,0:T(8,128)} %copy.8.weight_ref, bf16[1,1,7168,256]{3,2,1,0:T(8,128)(2,1)} %gate_hbm.1, bf16[1,1,7168,256]{3,2,1,0:T(8,128)(2,1)} %up_hbm.1, bf16[1,1,256,7168]{3,2,1,0:T(8,128)(2,1)} %down_hbm.1), custom_call_target="tpu_custom_call" | custom-call | flops 5637144576 | bytes 11010048 | tf_op jit(solution)/shard_map/pallas_call | solution.py:438
  88.2 1.6 %copy.10 = bf16[16,7168]{1,0:T(8,128)(2,1)} copy(bf16[16,7168]{1,0:T(8,128)(2,1)} %shard_map.64) | data formatting | bytes 458752

commit v2 on v1

--- a/solution.py
+++ b/solution.py
@@ -119,12 +119,21 @@
 
     own = band(rail * node_size + node)
     rows_ref[own, plain] = tokens_ref[...]
-    lane = lax.broadcasted_iota(jnp.int32, (count, LANES), 1)
-    named = jnp.zeros((count, LANES), jnp.float32)
-    for k in range(routes_ref.shape[1]):
-        named += jnp.where(
-            lane == routes_ref[:, k : k + 1], weight_ref[:, k : k + 1].astype(jnp.float32), 0.0
-        )
+    kind = lax.broadcasted_iota(jnp.int32, (LANES, count), 0)
+    table = jnp.zeros((LANES, count), jnp.float32)
+    for k in range(routes_ref.shape[0]):
+        table += jnp.where(
+            kind == routes_ref[k : k + 1, :], weight_ref[k : k + 1, :].astype(jnp.float32), 0.0
+        )
+    unit = lax.broadcasted_iota(jnp.int32, (count, count), 0) == lax.broadcasted_iota(
+        jnp.int32, (count, count), 1
+    )
+    named = lax.dot_general(
+        unit.astype(jnp.bfloat16),
+        table.astype(jnp.bfloat16),
+        (((1,), (1,)), ((), ())),
+        preferred_element_type=jnp.float32,
+    )
     rows_ref[own, slice(width, width + LANES)] = named.astype(jnp.bfloat16)
     pl.semaphore_wait(barrier, 3 + has_above.astype(jnp.int32) + has_below.astype(jnp.int32))
 
@@ -224,21 +233,109 @@
             relay_in(zz, h).wait_recv()
         sibling(index_of(zz, 1, 1)).start()
 
-    def gather_step(t, carry):
-        visit(t, gather_a)
-
-        @pl.when(t == 0)
-        def _():
-            for load in loads:
-                load.start()
-
-        visit(t - 2, gather_b)
-        visit(t - 4, gather_c)
-        return carry
-
-    lax.fori_loop(0, steps + 4, gather_step, 0)
-
-    def gather_end(zz, carry):
+    def give(r):
+        return copy(
+            rows_at(r, 1 - node, plain),
+            sib_buf.at[band(r), :],
+            give_send.at[r],
+            give_recv.at[r],
+            to_sib,
+        )
+
+    def side(r, h):
+        return copy(
+            rows_at(r, node, halves[h]),
+            side_buf.at[band(r), halves[h]],
+            side_send.at[r, h],
+            side_recv.at[r, h],
+            (to_y, to_x)[h],
+        )
+
+    def line(zz, h):
+        return copy(
+            rows_at(index_of(zz, h == 0, h == 1), node, halves[h]),
+            line_buf.at[band(zz), halves[h]],
+            line_send.at[zz, h],
+            line_recv.at[zz, h],
+            (to_x, to_y)[h],
+        )
+
+    def sum_up(zz):
+        return copy(
+            rows_at(index_of(zz, 0, 0), node, plain),
+            above_buf.at[band(zz), :],
+            sum_send.at[zz],
+            above_recv.at[zz],
+            to_above,
+        )
+
+    def sum_down(zz):
+        return copy(
+            rows_at(index_of(zz, 0, 0), node, plain),
+            below_buf.at[band(zz), :],
+            sum_send.at[zz],
+            below_recv.at[zz],
+            to_below,
+        )
+
+    def add(r, columns, other):
+        where = band(r * node_size + node)
+        rows_ref[where, columns] = (
+            rows_ref[where, columns].astype(jnp.float32) + other.astype(jnp.float32)
+        ).astype(jnp.bfloat16)
+
+    corners = ((1, 1), (0, 1), (1, 0), (0, 0))
+
+    def reduce_0(zz):
+        for fx, fy in corners:
+            give(index_of(zz, fx, fy)).start()
+
+    def reduce_a(zz):
+        for fx, fy in corners:
+            r = index_of(zz, fx, fy)
+            give(r).wait_recv()
+            add(r, plain, sib_buf[band(r), :])
+            if fy:
+                side(r, 0).start()
+            if fx:
+                side(r, 1).start()
+
+    def reduce_b(zz):
+        for h in range(2):
+            r = index_of(zz, h == 0, h == 1)
+            side(r, h).wait_recv()
+            add(r, halves[h], side_buf[band(r), halves[h]])
+            line(zz, h).start()
+        r = index_of(zz, 0, 0)
+        for h in range(2):
+            side(r, h).wait_recv()
+            add(r, halves[h], side_buf[band(r), halves[h]])
+
+    def reduce_c(zz):
+        for h in range(2):
+            line(zz, h).wait_recv()
+        r = index_of(zz, 0, 0)
+        add(r, plain, line_buf[band(zz), :])
+
+        @pl.when((zz >= z) & has_below)
+        def _():
+            sum_up(zz).wait_recv()
+            add(r, plain, above_buf[band(zz), :])
+
+        @pl.when((zz <= z) & has_above)
+        def _():
+            sum_down(zz).wait_recv()
+            add(r, plain, below_buf[band(zz), :])
+
+        @pl.when(zz > z)
+        def _():
+            sum_up(zz).start()
+
+        @pl.when(zz < z)
+        def _():
+            sum_down(zz).start()
+
+    def settle(zz):
         @pl.when((zz <= z) & has_above)
         def _():
             chain_up(zz).wait_send()
@@ -251,22 +348,16 @@
             first(zz, h).wait_send()
             second(zz, h).wait_send()
             relay(zz, h).wait_send()
-        for fx, fy in ((0, 0), (0, 1), (1, 0), (1, 1)):
+        for fx, fy in corners:
             r = index_of(zz, fx, fy)
             sibling(r).wait_send()
             sibling_in(r).wait_recv()
-        return carry
-
-    lax.fori_loop(0, depth, gather_end, 0)
-    for load in loads:
-        load.wait()
-
-    total = rail_size * node_size * count
-    chunk = min(128, total)
+
+    chunk = SQUARE * node_size * count
     column_step = next(s for s in (1792, 1024, 512, 256, 128) if width % s == 0)
 
-    def compute(i, carry):
-        here = pl.ds(pl.multiple_of(i * chunk, chunk), chunk)
+    def compute(zz):
+        here = pl.ds(pl.multiple_of(zz * chunk, chunk), chunk)
         lane = lax.broadcasted_iota(jnp.int32, (chunk, LANES), 1)
         marks = rows_ref[here, slice(width, width + LANES)].astype(jnp.float32)
         share = jnp.sum(jnp.where(lane == expert, marks, 0.0), axis=1, keepdims=True) / 256.0
@@ -280,117 +371,32 @@
             rows_ref[here, columns] = jnp.dot(
                 hidden, down_ref[:, columns], preferred_element_type=jnp.float32
             ).astype(jnp.bfloat16)
+
+    def expert_rows(zz):
+        settle(zz)
+        compute(zz)
+        reduce_0(zz)
+
+    def gather_step(t, carry):
+        visit(t, gather_a)
+
+        @pl.when(t == 0)
+        def _():
+            for load in loads:
+                load.start()
+
+        visit(t - 1, gather_b)
+        visit(t - 3, gather_c)
+
+        @pl.when(t == 5)
+        def _():
+            for load in loads:
+                load.wait()
+
+        visit(t - 5, expert_rows)
         return carry
 
-    lax.fori_loop(0, total // chunk, compute, 0)
-
-    def give(r):
-        return copy(
-            rows_at(r, 1 - node, plain),
-            sib_buf.at[band(r), :],
-            give_send.at[r],
-            give_recv.at[r],
-            to_sib,
-        )
-
-    def side(r, h):
-        return copy(
-            rows_at(r, node, halves[h]),
-            side_buf.at[band(r), halves[h]],
-            side_send.at[r, h],
-            side_recv.at[r, h],
-            (to_y, to_x)[h],
-        )
-
-    def line(zz, h):
-        return copy(
-            rows_at(index_of(zz, h == 0, h == 1), node, halves[h]),
-            line_buf.at[band(zz), halves[h]],
-            line_send.at[zz, h],
-            line_recv.at[zz, h],
-            (to_x, to_y)[h],
-        )
-
-    def sum_up(zz):
-        return copy(
-            rows_at(index_of(zz, 0, 0), node, plain),
-            above_buf.at[band(zz), :],
-            sum_send.at[zz],
-            above_recv.at[zz],
-            to_above,
-        )
-
-    def sum_down(zz):
-        return copy(
-            rows_at(index_of(zz, 0, 0), node, plain),
-            below_buf.at[band(zz), :],
-            sum_send.at[zz],
-            below_recv.at[zz],
-            to_below,
-        )
-
-    def add(r, columns, other):
-        where = band(r * node_size + node)
-        rows_ref[where, columns] = (
-            rows_ref[where, columns].astype(jnp.float32) + other.astype(jnp.float32)
-        ).astype(jnp.bfloat16)
-
-    corners = ((1, 1), (0, 1), (1, 0), (0, 0))
-
-    def reduce_0(zz):
-        for fx, fy in corners:
-            give(index_of(zz, fx, fy)).start()
-
-    def reduce_a(zz):
-        for fx, fy in corners:
-            r = index_of(zz, fx, fy)
-            give(r).wait_recv()
-            add(r, plain, sib_buf[band(r), :])
-            if fy:
-                side(r, 0).start()
-            if fx:
-                side(r, 1).start()
-
-    def reduce_b(zz):
-        for h in range(2):
-            r = index_of(zz, h == 0, h == 1)
-            side(r, h).wait_recv()
-            add(r, halves[h], side_buf[band(r), halves[h]])
-            line(zz, h).start()
-        r = index_of(zz, 0, 0)
-        for h in range(2):
-            side(r, h).wait_recv()
-            add(r, halves[h], side_buf[band(r), halves[h]])
-
-    def reduce_c(zz):
-        for h in range(2):
-            line(zz, h).wait_recv()
-        r = index_of(zz, 0, 0)
-        add(r, plain, line_buf[band(zz), :])
-
-        @pl.when((zz >= z) & has_below)
-        def _():
-            sum_up(zz).wait_recv()
-            add(r, plain, above_buf[band(zz), :])
-
-        @pl.when((zz <= z) & has_above)
-        def _():
-            sum_down(zz).wait_recv()
-            add(r, plain, below_buf[band(zz), :])
-
-        @pl.when(zz > z)
-        def _():
-            sum_up(zz).start()
-
-        @pl.when(zz < z)
-        def _():
-            sum_down(zz).start()
-
-    def reduce_0_step(t, carry):
-        visit(steps - 1 - t, reduce_0)
-        return carry
-
-    lax.fori_loop(0, steps, reduce_0_step, 0)
+    lax.fori_loop(0, steps + 5, gather_step, 0)
 
     def reduce_step(t, carry):
         q = steps - 1 - t
@@ -479,7 +485,7 @@
             bytes_accessed=6 * width * hidden,
             transcendentals=total * hidden,
         ),
-    )(tokens, routes, route_weight, gate, up, down)
+    )(tokens, routes.T, route_weight.T, gate, up, down)
 
 
 def solution(mesh):

time: 90 us -> 84.5 us (0.939)
  Pallas kernels: 85.4 us -> 82.5 us
  local copies, waits for them, and re-layouts: 4.34 us -> 1.64 us
    pallas_call x1, Pallas kernels: 85.4 us -> 82.5 us  [shards(): pl.pallas_call(functools.partial(body, rail_size, node_size), out_shape=j...]
    unnamed x3 -> x1, local copies, waits for them, and re-layouts: 4.34 us -> 1.64 us
where the time goes in v2:
time: 84.5 us; the launch traced here: 84.1 us
  Pallas kernels  82.5 us (98%)
  local copies, waits for them, and re-layouts  1.64 us (2%)
    pallas_call x1, Pallas kernels, shards(): pl.pallas_call(functools.partial(body, rail_size, node_size), out_shape=j...  82.5 us

profile of v2, /device:TPU:0, one launch (start us, length us, event | category | flops | bytes accessed | tf_op | source)
XLA Modules:
  0.0 84.1 jit_solution(6834956109498590808)
XLA Ops:
  0.0 82.5 %shard_map.64 = bf16[16,7168]{1,0:T(8,128)(2,1)} custom-call(bf16[16,7168]{1,0:T(8,128)(2,1)} %tokens_ref.1, s32[2,16]{1,0:T(2,128)} %bitcast.2, s32[2,16]{1,0:T(2,128)} %bitcast.3, bf16[1,1,7168,256]{3,2,1,0:T(8,128)(2,1)} %gate_hbm.1, bf16[1,1,7168,256]{3,2,1,0:T(8,128)(2,1)} %up_hbm.1, bf16[1,1,256,7168]{3,2,1,0:T(8,128)(2,1)} %down_hbm.1), custom_call_target="tpu_custom_call" | custom-call | flops 5637144576 | bytes 11010048 | tf_op jit(solution)/shard_map/pallas_call | solution.py:444
  82.5 1.6 %copy.8 = bf16[16,7168]{1,0:T(8,128)(2,1)} copy(bf16[16,7168]{1,0:T(8,128)(2,1)} %shard_map.64) | data formatting | bytes 458752

commit v3 on v2

--- a/solution.py
+++ b/solution.py
@@ -401,8 +401,8 @@
     def reduce_step(t, carry):
         q = steps - 1 - t
         visit(q, reduce_a)
+        visit(q + 4, reduce_c)
         visit(q + 2, reduce_b)
-        visit(q + 4, reduce_c)
         return carry
 
     lax.fori_loop(0, steps + 4, reduce_step, 0)

time: 84.5 us -> 84.5 us (level)
  no operation moved by 1% of the time
where the time goes in v3:
time: 84.5 us; the launch traced here: 84.1 us
  Pallas kernels  82.5 us (98%)
  local copies, waits for them, and re-layouts  1.64 us (2%)
    pallas_call x1, Pallas kernels, shards(): pl.pallas_call(functools.partial(body, rail_size, node_size), out_shape=j...  82.5 us

profile of v3, /device:TPU:0, one launch (start us, length us, event | category | flops | bytes accessed | tf_op | source)
XLA Modules:
  0.0 84.1 jit_solution(2780757810300465407)
XLA Ops:
  0.0 82.5 %shard_map.64 = bf16[16,7168]{1,0:T(8,128)(2,1)} custom-call(bf16[16,7168]{1,0:T(8,128)(2,1)} %tokens_ref.1, s32[2,16]{1,0:T(2,128)} %bitcast.2, s32[2,16]{1,0:T(2,128)} %bitcast.3, bf16[1,1,7168,256]{3,2,1,0:T(8,128)(2,1)} %gate_hbm.1, bf16[1,1,7168,256]{3,2,1,0:T(8,128)(2,1)} %up_hbm.1, bf16[1,1,256,7168]{3,2,1,0:T(8,128)(2,1)} %down_hbm.1), custom_call_target="tpu_custom_call" | custom-call | flops 5637144576 | bytes 11010048 | tf_op jit(solution)/shard_map/pallas_call | solution.py:444
  82.5 1.6 %copy.8 = bf16[16,7168]{1,0:T(8,128)(2,1)} copy(bf16[16,7168]{1,0:T(8,128)(2,1)} %shard_map.64) | data formatting | bytes 458752
